TPU v7x, 32 devices: a whole 2x2x4 slice. The times are simulated.
32 devices in a mesh: layer: 2 (over core), row: 4 (over y, x), col: 4 (over z).
Axes of the slice: x: 2, y: 2, z: 4, core: 2. Of those that a mesh axis runs over, the one named last changes fastest.
Arguments:
- rhs_sub: float32 [2, 3, 1, 4, 256, 512], P('layer', None, None, 'row', 'col'), may hold values from -6 to 6
- rhs_top: float32 [1, 4, 256, 512], P(None, 'row', 'col'), may hold values from -6 to 6
- lower_inv_sub: float32 [2, 3, 1, 4, 256, 256], P('layer', None, None, 'row', 'col'), as said below
- lower_inv_top: float32 [1, 4, 256, 256], P(None, 'row', 'col'), as said below
- upper_inv_sub: float32 [2, 3, 1, 4, 256, 256], P('layer', None, None, 'row', 'col'), as said below
- upper_inv_top: float32 [1, 4, 256, 256], P(None, 'row', 'col'), as said below
- lower_sub: float32 [2, 3, 1, 4, 1, 4, 256, 256], P('layer', None, None, 'row', None, 'col'), may hold values from -0.1875 to 0.1875
- lower_top: float32 [2, 3, 1, 4, 1, 4, 256, 256], P('layer', None, None, 'row', None, 'col'), may hold values from -0.109375 to 0.109375
- upper_sub: float32 [2, 3, 1, 4, 1, 4, 256, 256], P('layer', None, None, 'row', None, 'col'), may hold values from -0.125 to 0.125
- upper_top: float32 [2, 3, 1, 4, 1, 4, 256, 256], P('layer', None, None, 'row', None, 'col'), may hold values from -0.1875 to 0.1875
- block_pattern: int32 [2, 4, 3, 1, 4, 1, 4], P('layer', None, None, None, 'row', None, 'col'), may hold values 0 or 1
Outputs:
- solution_sub: float32 [2, 3, 1, 4, 256, 512], P('layer', None, None, 'row', 'col')
- solution_top: float32 [1, 4, 256, 512], P(None, 'row', 'col')
Inputs may be any that keep to these rules, and one draw needn't show every extreme that they name: `lower_inv_sub`: every 256 x 256 block is lower triangular with unit diagonal. `lower_inv_top`: every 256 x 256 block is lower triangular with unit diagonal. `upper_inv_sub`: every 256 x 256 block is upper triangular with unit diagonal. `upper_inv_top`: every 256 x 256 block is upper triangular with unit diagonal.
All inputs are finite; a program needn't handle non-finite values. No bound on the sum of `block_pattern` on one device may be relied on, other than what follows from the above.
Results may differ from a plain program's by a relative error of at most 0.00014.
Values sent between devices are 32-bit elements; how exact they have to be, the bound alone decides.
A program may use at most 64 MiB of HBM per device.

v0:
```python
import jax
import jax.numpy as jnp
from jax import lax
from jax.sharding import PartitionSpec as P

HIGHEST = lax.Precision.HIGHEST


def broadcast(x, axis, root):
    mine = lax.axis_index(axis) == root
    return lax.psum(jnp.where(mine, x, jnp.zeros_like(x)), axis)


def couple(blocks, pattern, solution):
    weighted = solution[None] * pattern[:, :, None, None].astype(jnp.float32)
    return jnp.einsum("tsab,tsbn->tan", blocks, weighted, precision=HIGHEST)


def spread(whole_block):
    return broadcast(whole_block, "row", lax.axis_index("col"))


def on_device(
    rhs_sub,
    rhs_top,
    lower_inv_sub,
    lower_inv_top,
    upper_inv_sub,
    upper_inv_top,
    lower_sub,
    lower_top,
    upper_sub,
    upper_top,
    block_pattern,
):
    column = lax.axis_index("col")
    width_rows = rhs_top.shape[2]
    gathered = (
        lax.all_gather(lower_inv_sub, "col", axis=4, tiled=True),
        lax.all_gather(lower_inv_top, "col", axis=2, tiled=True),
        lax.all_gather(upper_inv_sub, "col", axis=4, tiled=True),
        lax.all_gather(upper_inv_top, "col", axis=2, tiled=True),
        lax.all_gather(rhs_sub, "col", axis=4, tiled=True),
        lax.all_gather(rhs_top, "col", axis=2, tiled=True),
    )
    lower_list = [gathered[0][0, level, :, 0] for level in range(3)] + [gathered[1][:, 0]]
    upper_list = [gathered[2][0, level, :, 0] for level in range(3)] + [gathered[3][:, 0]]
    right_sides = [gathered[4][0, level, :, 0] for level in range(3)] + [gathered[5][:, 0]]

    def solve(partial_value, right_side, inverse_full, top):
        if partial_value is None:
            residual = right_side
        elif top:
            residual = right_side - lax.psum(partial_value, ("layer", "col"))
        else:
            residual = right_side - lax.psum(partial_value, "col")
        return jnp.einsum("kab,kbn->kan", inverse_full, residual, precision=HIGHEST)

    def copy_out(solution):
        return spread(solution)

    def keep_rows(solution):
        return lax.dynamic_slice_in_dim(solution, column * width_rows, width_rows, 1)

    def blocks(array, pair):
        return array[0, pair, :, 0, :, 0]

    def pattern(kind, pair):
        return block_pattern[0, kind, pair, :, 0, :, 0]

    fore_zero = solve(None, right_sides[0], lower_list[0], False)
    copy_zero = copy_out(fore_zero)
    into_one = couple(blocks(lower_sub, 0), pattern(0, 0), copy_zero)
    into_two = couple(blocks(lower_sub, 1), pattern(0, 1), copy_zero)
    into_top = couple(blocks(lower_top, 0), pattern(1, 0), copy_zero)
    fore_one = solve(into_one, right_sides[1], lower_list[1], False)
    copy_one = copy_out(fore_one)
    into_two = into_two + couple(blocks(lower_sub, 2), pattern(0, 2), copy_one)
    into_top = into_top + couple(blocks(lower_top, 1), pattern(1, 1), copy_one)
    fore_two = solve(into_two, right_sides[2], lower_list[2], False)
    copy_two = copy_out(fore_two)
    into_top = into_top + couple(blocks(lower_top, 2), pattern(1, 2), copy_two)
    fore_top = solve(into_top, right_sides[3], lower_list[3], True)
    final_top = solve(None, fore_top, upper_list[3], False)
    down_top = copy_out(final_top)
    toward_two = couple(blocks(upper_top, 2), pattern(3, 2), down_top)
    toward_one = couple(blocks(upper_top, 1), pattern(3, 1), down_top)
    toward_zero = couple(blocks(upper_top, 0), pattern(3, 0), down_top)
    final_two = solve(toward_two, fore_two, upper_list[2], False)
    down_two = copy_out(final_two)
    toward_one = toward_one + couple(blocks(upper_sub, 2), pattern(2, 2), down_two)
    toward_zero = toward_zero + couple(blocks(upper_sub, 1), pattern(2, 1), down_two)
    final_one = solve(toward_one, fore_one, upper_list[1], False)
    down_one = copy_out(final_one)
    toward_zero = toward_zero + couple(blocks(upper_sub, 0), pattern(2, 0), down_one)
    final_zero = solve(toward_zero, fore_zero, upper_list[0], False)
    solution_sub = jnp.stack([keep_rows(final_zero), keep_rows(final_one), keep_rows(final_two)])[
        None, :, :, None
    ]
    solution_top = keep_rows(final_top)[:, None]
    return (solution_sub, solution_top)


def solution(mesh):
    placed = (
        P("layer", None, None, "row", "col", None),
        P(None, "row", "col", None),
        P("layer", None, None, "row", "col", None),
        P(None, "row", "col", None),
        P("layer", None, None, "row", "col", None),
        P(None, "row", "col", None),
        P("layer", None, None, "row", None, "col", None, None),
        P("layer", None, None, "row", None, "col", None, None),
        P("layer", None, None, "row", None, "col", None, None),
        P("layer", None, None, "row", None, "col", None, None),
        P("layer", None, None, None, "row", None, "col"),
    )
    return jax.shard_map(
        on_device,
        mesh=mesh,
        in_specs=placed,
        out_specs=(P("layer", None, None, "row", "col", None), P(None, "row", "col", None)),
        check_vma=False,
    )
```

profile of v0, /device:TPU:0, one launch (start us, length us, event | category | flops | bytes accessed | tf_op | source)
XLA Modules:
  0.0 627.9 jit_solution(5425671414691437283)
XLA Ops:
  7.2 2.1 copy.24
  9.4 26.4 %all_gather.18 = f32[1,3,1,1,256,256]{5,4,3,2,1,0:T(8,128)S(1)} all-gather(f32[1,3,1,1,64,256]{5,4,3,2,1,0:T(8,128)} %param.13), channel_id=1, replica_groups=mesh['layer'=2,'row'=4,'col'=4] {'col'}, dimensions={4}, use_global_device_ids=true | all-gather | bytes 983040 | tf_op jit(solution)/shard_map/all_gather | solution.py:39
  35.9 18.7 %all-gather.2.cloned.1.call-done = f32[1,3,1,1,256,512]{5,3,2,1,0,4:T(1,128)} async-done(((f32[1,3,1,1,64,512]{5,3,2,1,0,4:T(1,128)}), f32[1,3,1,1,256,512]{5,3,2,1,0,4:T(1,128)}) %all-gather.2.cloned.1.call-update) | async-done | bytes 1572880 | tf_op jit(solution)/shard_map/all_gather | solution.py:43
  54.6 3.2 fusion.90
  58.4 0.8 select_bitcast_fusion.3
  60.7 44.4 %all-reduce.13.cloned.1.call-done = f32[1,256,512]{2,1,0:T(8,128)} async-done(((f32[1,256,512]{2,1,0:T(8,128)}), f32[1,256,512]{2,1,0:T(8,128)}) %all-reduce.13.cloned.1.call-update) | async-done | bytes 524304 | tf_op jit(solution)/shard_map/psum | solution.py:11
  105.2 2.9 convolution_bitcast_fusion.1
  108.7 37.9 %all-reduce.15.cloned.1.call-done = f32[1,256,512]{1,2,0:T(8,128)} async-done(((f32[1,256,512]{1,2,0:T(8,128)}), f32[1,256,512]{1,2,0:T(8,128)}) %all-reduce.15.cloned.1.call-update) | async-done | bytes 524304 | tf_op jit(solution)/shard_map/psum | solution.py:56
  146.6 1.7 fusion.34
  148.3 0.9 fusion.33
  150.5 2.0 fusion.30
  152.5 42.3 %all-reduce.17.cloned.1.call-done = f32[1,256,512]{2,1,0:T(8,128)} async-done(((f32[1,256,512]{2,1,0:T(8,128)}), f32[1,256,512]{2,1,0:T(8,128)}) %all-reduce.17.cloned.1.call-update) | async-done | bytes 524304 | tf_op jit(solution)/shard_map/psum | solution.py:11
  194.8 2.9 fusion.3
  199.7 1.2 copy.48
  200.9 35.2 %all-reduce.19.cloned.1.call-done = f32[1,256,512]{1,2,0:T(8,128)} async-done(((f32[1,256,512]{1,2,0:T(8,128)}), f32[1,256,512]{1,2,0:T(8,128)}) %all-reduce.19.cloned.1.call-update) | async-done | bytes 524304 | tf_op jit(solution)/shard_map/psum | solution.py:56
  236.1 1.7 fusion.27
  237.9 0.9 fusion.26
  238.8 2.0 fusion.37
  240.8 2.0 convolution_add_fusion.5
  242.7 41.6 %all-reduce.21.cloned.1.call-done = f32[1,256,512]{2,1,0:T(8,128)} async-done(((f32[1,256,512]{2,1,0:T(8,128)}), f32[1,256,512]{2,1,0:T(8,128)}) %all-reduce.21.cloned.1.call-update) | async-done | bytes 524304 | tf_op jit(solution)/shard_map/psum | solution.py:11
  284.4 2.9 fusion.2
  287.3 17.9 %all_gather.20 = f32[1,1,256,512]{3,1,0,2:T(1,128)S(1)} all-gather(f32[1,1,64,512]{3,1,0,2:T(1,128)S(1)} %copy.25), channel_id=1, replica_groups=mesh['layer'=2,'row'=4,'col'=4] {'col'}, dimensions={2}, use_global_device_ids=true | all-gather | bytes 655360 | tf_op jit(solution)/shard_map/all_gather | solution.py:44
  305.7 14.3 %all_gather.21 = f32[1,1,256,256]{3,2,1,0:T(8,128)S(1)} all-gather(f32[1,1,64,256]{3,2,1,0:T(8,128)S(1)} %copy-done.6), channel_id=1, replica_groups=mesh['layer'=2,'row'=4,'col'=4] {'col'}, dimensions={2}, use_global_device_ids=true | all-gather | bytes 327680 | tf_op jit(solution)/shard_map/all_gather | solution.py:40
  320.0 14.6 %all_gather.22 = f32[1,1,256,256]{3,2,1,0:T(8,128)S(1)} all-gather(f32[1,1,64,256]{3,2,1,0:T(8,128)S(1)} %copy-done.7), channel_id=1, replica_groups=mesh['layer'=2,'row'=4,'col'=4] {'col'}, dimensions={2}, use_global_device_ids=true | all-gather | bytes 327680 | tf_op jit(solution)/shard_map/all_gather | solution.py:42
  334.6 10.1 %all-reduce.23.cloned.1.call-done = f32[1,256,512]{1,2,0:T(8,128)} async-done(((f32[1,256,512]{1,2,0:T(8,128)}), f32[1,256,512]{1,2,0:T(8,128)}) %all-reduce.23.cloned.1.call-update) | async-done | bytes 524304 | tf_op jit(solution)/shard_map/psum | solution.py:54
  344.7 1.7 fusion.23
  347.1 0.8 copy-done.2
  347.9 0.8 select_bitcast_fusion.2
  349.5 43.6 %all-reduce.25.cloned.1.call-done = f32[1,256,512]{2,1,0:T(8,128)} async-done(((f32[1,256,512]{2,1,0:T(8,128)}), f32[1,256,512]{2,1,0:T(8,128)}) %all-reduce.25.cloned.1.call-update) | async-done | bytes 524304 | tf_op jit(solution)/shard_map/psum | solution.py:11
  393.1 2.6 convolution_bitcast_fusion
  395.7 27.4 %all_gather.23 = f32[1,3,1,1,256,256]{5,4,3,2,1,0:T(8,128)S(1)} all-gather(f32[1,3,1,1,64,256]{5,4,3,2,1,0:T(8,128)S(1)} %copy-done.4), channel_id=1, replica_groups=mesh['layer'=2,'row'=4,'col'=4] {'col'}, dimensions={4}, use_global_device_ids=true | all-gather | bytes 983040 | tf_op jit(solution)/shard_map/all_gather | solution.py:41
  423.1 16.7 %all-reduce.27.cloned.1.call-done = f32[1,256,512]{2,1,0:T(8,128)} async-done(((f32[1,256,512]{2,1,0:T(8,128)}), f32[1,256,512]{2,1,0:T(8,128)}) %all-reduce.27.cloned.1.call-update) | async-done | bytes 524304 | tf_op jit(solution)/shard_map/psum | solution.py:56
  439.8 1.7 fusion.11
  441.5 0.8 select_bitcast_fusion.1
  443.7 1.6 fusion.17
  445.3 43.0 %all-reduce.29.cloned.1.call-done = f32[1,256,512]{2,1,0:T(8,128)} async-done(((f32[1,256,512]{2,1,0:T(8,128)}), f32[1,256,512]{2,1,0:T(8,128)}) %all-reduce.29.cloned.1.call-update) | async-done | bytes 524304 | tf_op jit(solution)/shard_map/psum | solution.py:11
  488.3 2.6 fusion.1
  492.8 36.6 %all-reduce.31.cloned.1.call-done = f32[1,256,512]{2,1,0:T(8,128)} async-done(((f32[1,256,512]{2,1,0:T(8,128)}), f32[1,256,512]{2,1,0:T(8,128)}) %all-reduce.31.cloned.1.call-update) | async-done | bytes 524304 | tf_op jit(solution)/shard_map/psum | solution.py:56
  529.4 1.7 fusion.8
  531.1 0.8 select_bitcast_fusion
  532.0 1.6 fusion.21
  533.6 1.8 convolution_add_fusion.2
  535.4 42.5 %all-reduce.33.cloned.1.call-done = f32[1,256,512]{2,1,0:T(8,128)} async-done(((f32[1,256,512]{2,1,0:T(8,128)}), f32[1,256,512]{2,1,0:T(8,128)}) %all-reduce.33.cloned.1.call-update) | async-done | bytes 524304 | tf_op jit(solution)/shard_map/psum | solution.py:11
  577.9 2.6 fusion
  580.4 1.6 dynamic-slice_bitcast_fusion
  582.1 36.8 %all-reduce.35.cloned.1.call-done = f32[1,256,512]{2,1,0:T(8,128)} async-done(((f32[1,256,512]{2,1,0:T(8,128)}), f32[1,256,512]{2,1,0:T(8,128)}) %all-reduce.35.cloned.1.call-update) | async-done | bytes 524304 | tf_op jit(solution)/shard_map/psum | solution.py:56
  618.9 1.7 fusion.13
  620.6 0.8 maximum_bitcast_fusion
  (52 shorter events, 3.9 us)
Async XLA Ops:
  7.2 47.4 %all-gather.2.cloned.1.call-start = ((), (), s32[]{:S(2)}) async-start(), calls=%async_computation | async-start | bytes 1966080 | tf_op jit(solution)/shard_map/all_gather | solution.py:43
  9.4 95.8 %all-reduce.13.cloned.1.call-start = ((), (), s32[]{:S(2)}) async-start(), calls=%async_computation.1 | async-start | bytes 1048576 | tf_op jit(solution)/shard_map/psum | solution.py:11
  57.8 1.5 copy-start.8
  59.3 87.3 %all-reduce.15.cloned.1.call-start = ((), (), s32[]{:S(2)}) async-start(), calls=%async_computation.2 | async-start | bytes 1048576 | tf_op jit(solution)/shard_map/psum | solution.py:56
  108.1 86.7 %all-reduce.17.cloned.1.call-start = ((), (), s32[]{:S(2)}) async-start(), calls=%async_computation.3 | async-start | bytes 1048576 | tf_op jit(solution)/shard_map/psum | solution.py:11
  108.7 41.8 %copy-start = (f32[1,256,512]{2,1,0:T(8,128)S(1)}, f32[1,256,512]{2,1,0:T(8,128)}, u32[]{:S(2)}) copy-start(f32[1,256,512]{2,1,0:T(8,128)} %all-reduce.13.cloned.1.call-done) | copy-start | bytes 1572868
  149.2 87.0 %all-reduce.19.cloned.1.call-start = ((), (), s32[]{:S(2)}) async-start(), calls=%async_computation.4 | async-start | bytes 1048576 | tf_op jit(solution)/shard_map/psum | solution.py:56
  150.5 49.1 %copy-start.5 = (f32[1,1,64,512]{3,2,1,0:T(8,128)S(1)}, f32[1,1,64,512]{3,2,1,0:T(8,128)}, u32[]{:S(2)}) copy-start(f32[1,1,64,512]{3,2,1,0:T(8,128)} %param.12) | copy-start | bytes 393220
  197.7 86.7 %all-reduce.21.cloned.1.call-start = ((), (), s32[]{:S(2)}) async-start(), calls=%async_computation.5 | async-start | bytes 1048576 | tf_op jit(solution)/shard_map/psum | solution.py:11
  237.9 2.9 copy-start.3
  238.8 106.0 %all-reduce.23.cloned.1.call-start = ((), (), s32[]{:S(2)}) async-start(), calls=%async_computation.6 | async-start | bytes 1048576 | tf_op jit(solution)/shard_map/psum | solution.py:54
  287.3 18.4 %copy-start.6 = (f32[1,1,64,256]{3,2,1,0:T(8,128)S(1)}, f32[1,1,64,256]{3,2,1,0:T(8,128)}, u32[]{:S(2)}) copy-start(f32[1,1,64,256]{3,2,1,0:T(8,128)} %param.14) | copy-start | bytes 196612
  287.3 32.8 %copy-start.7 = (f32[1,1,64,256]{3,2,1,0:T(8,128)S(1)}, f32[1,1,64,256]{3,2,1,0:T(8,128)}, u32[]{:S(2)}) copy-start(f32[1,1,64,256]{3,2,1,0:T(8,128)} %param.16) | copy-start | bytes 196612
  287.3 105.8 %all-reduce.25.cloned.1.call-start = ((), (), s32[]{:S(2)}) async-start(), calls=%async_computation.7 | async-start | bytes 1048576 | tf_op jit(solution)/shard_map/psum | solution.py:11
  347.1 0.8 copy-start.2
  347.9 47.9 %copy-start.4 = (f32[1,3,1,1,64,256]{5,4,3,2,1,0:T(8,128)S(1)}, f32[1,3,1,1,64,256]{5,4,3,2,1,0:T(8,128)}, u32[]{:S(2)}) copy-start(f32[1,3,1,1,64,256]{5,4,3,2,1,0:T(8,128)} %param.15) | copy-start | bytes 589828
  348.7 91.1 %all-reduce.27.cloned.1.call-start = ((), (), s32[]{:S(2)}) async-start(), calls=%async_computation.8 | async-start | bytes 1048576 | tf_op jit(solution)/shard_map/psum | solution.py:56
  395.7 92.7 %all-reduce.29.cloned.1.call-start = ((), (), s32[]{:S(2)}) async-start(), calls=%async_computation.9 | async-start | bytes 1048576 | tf_op jit(solution)/shard_map/psum | solution.py:11
  423.1 20.6 %copy-start.1 = (f32[1,256,512]{2,1,0:T(8,128)S(1)}, f32[1,256,512]{2,1,0:T(8,128)}, u32[]{:S(2)}) copy-start(f32[1,256,512]{2,1,0:T(8,128)} %all-reduce.25.cloned.1.call-done) | copy-start | bytes 1572868
  442.4 87.0 %all-reduce.31.cloned.1.call-start = ((), (), s32[]{:S(2)}) async-start(), calls=%async_computation.10 | async-start | bytes 1048576 | tf_op jit(solution)/shard_map/psum | solution.py:56
  490.9 86.9 %all-reduce.33.cloned.1.call-start = ((), (), s32[]{:S(2)}) async-start(), calls=%async_computation.11 | async-start | bytes 1048576 | tf_op jit(solution)/shard_map/psum | solution.py:11
  531.9 87.0 %all-reduce.35.cloned.1.call-start = ((), (), s32[]{:S(2)}) async-start(), calls=%async_computation.12 | async-start | bytes 1048576 | tf_op jit(solution)/shard_map/psum | solution.py:56
Sparse Core Ops, SparseCore 0:
  10.1 44.3 all-gather.1
  59.4 45.7 all-reduce.12
  108.2 38.2 all-reduce.14
  149.4 45.3 all-reduce.16
  197.8 38.2 all-reduce.18
  239.0 45.3 all-reduce.20
  287.4 57.2 all-reduce.22
  348.8 44.1 all-reduce.24
  395.8 44.0 all-reduce.26
  442.9 45.3 all-reduce.28
  491.0 38.2 all-reduce.30
  532.5 45.3 all-reduce.32
  580.6 38.2 all-reduce.34
where the time goes:
time: 629 us; the launch traced here: 628 us
  waiting for transfers between devices  450 us (72%)
  blocking collectives  101 us (16%)
  matrix products  38.7 us (6%)
  between operations  21.7 us (3%)
  local copies, waits for them, and re-layouts  10.9 us (2%)
    psum x6, waiting for transfers between devices, broadcast(): return lax.psum(jnp.where(mine, x, jnp.zeros_like(x)), axis)  257 us
    psum x5, waiting for transfers between devices, solve(): residual = right_side - lax.psum(partial_value, 'col')  163 us
    all_gather x1, blocking collectives, on_device(): lax.all_gather(upper_inv_sub, 'col', axis=4, tiled=True)  27.4 us
    dot_general x12, matrix products, couple(): return jnp.einsum('tsab,tsbn->tan', blocks, weighted, precision=HIGHEST)  27.3 us
    all_gather x1, blocking collectives, on_device(): lax.all_gather(lower_inv_sub, 'col', axis=4, tiled=True)  26.4 us
    all_gather x1, waiting for transfers between devices, on_device(): lax.all_gather(rhs_sub, 'col', axis=4, tiled=True)  18.7 us
    all_gather x1, blocking collectives, on_device(): lax.all_gather(rhs_top, 'col', axis=2, tiled=True)  17.9 us
    all_gather x1, blocking collectives, on_device(): lax.all_gather(upper_inv_top, 'col', axis=2, tiled=True)  14.6 us
  transfers between devices with their start and end apart: 13, of which 13 were waited for; matrix products, arithmetic and copies ran while one was open for 2% of the time, Pallas kernels for 0%

commit v1 on v0

--- a/solution.py
+++ b/solution.py
@@ -1,9 +1,415 @@
+import functools
 import jax
 import jax.numpy as jnp
 from jax import lax
+from jax.experimental import pallas as pl
+from jax.experimental.pallas import tpu as pltpu
 from jax.sharding import PartitionSpec as P
 
 HIGHEST = lax.Precision.HIGHEST
+MESH = pl.DeviceIdType.MESH
+LEVELS = 3
+
+
+def dot(a, b):
+    return jnp.dot(a, b, precision=HIGHEST, preferred_element_type=jnp.float32)
+
+
+def kernel(
+    layers,
+    grid,
+    pattern,
+    rhs_sub,
+    rhs_top,
+    lower_inv_sub,
+    lower_inv_top,
+    upper_inv_sub,
+    upper_inv_top,
+    lower_sub,
+    lower_top,
+    upper_sub,
+    upper_top,
+    out_sub,
+    out_top,
+    coupling,
+    rhs_split,
+    rhs_stage,
+    rhs_full,
+    inv_stage,
+    inv_full,
+    part,
+    arrived,
+    solved,
+    cross,
+    out_stage,
+    out_full,
+    coupling_sem,
+    rhs_sem,
+    rhs_z_sem,
+    inv_sem,
+    inv_z_sem,
+    part_sem,
+    cross_sem,
+    out_z_sem,
+    out_sem,
+):
+    layer, row, col = lax.axis_index("layer"), lax.axis_index("row"), lax.axis_index("col")
+    width = part.shape[2]
+    columns = part.shape[3]
+    others = range(1, grid)
+
+    def ahead(me, step, count=grid):
+        return lax.rem(me + step, count)
+
+    barrier = pltpu.get_barrier_semaphore()
+    for step in others:
+        pl.semaphore_signal(barrier, inc=1, device_id=(layer, ahead(row, step), col), device_id_type=MESH)
+        pl.semaphore_signal(barrier, inc=1, device_id=(layer, row, ahead(col, step)), device_id_type=MESH)
+    for step in range(1, layers):
+        pl.semaphore_signal(
+            barrier, inc=1, device_id=(ahead(layer, step, layers), row, col), device_id_type=MESH
+        )
+
+    def remote(source, target, sems, index, step, device):
+        return pltpu.make_async_remote_copy(
+            src_ref=source,
+            dst_ref=target,
+            send_sem=sems.at[0, index, step - 1],
+            recv_sem=sems.at[1, index, step - 1],
+            device_id=device,
+            device_id_type=MESH,
+        )
+
+    sources = (
+        (lower_sub, 0, 0),
+        (lower_sub, 1, 0),
+        (lower_sub, 2, 0),
+        (lower_top, 0, 1),
+        (lower_top, 1, 1),
+        (lower_top, 2, 1),
+        (upper_top, 2, 3),
+        (upper_top, 1, 3),
+        (upper_sub, 2, 2),
+        (upper_top, 0, 3),
+        (upper_sub, 1, 2),
+        (upper_sub, 0, 2),
+    )
+    inverses = tuple(lower_inv_sub.at[k] for k in range(LEVELS)) + (lower_inv_top,)
+    inverses += tuple(upper_inv_sub.at[k] for k in range(LEVELS)) + (upper_inv_top,)
+    rights = tuple(rhs_sub.at[k] for k in range(LEVELS)) + (rhs_top,)
+
+    def mask(k):
+        ref, pair, kind = sources[k]
+        coupling[k, row] = ref[pair] * pattern[kind * LEVELS + pair].astype(jnp.float32)
+
+    def coupling_copy(k, step):
+        return remote(
+            coupling.at[k, row], coupling.at[k, row], coupling_sem, k, step, (layer, ahead(row, step), col)
+        )
+
+    def rhs_copy(k, step):
+        to = ahead(row, step)
+        return remote(rhs_split.at[k, to], rhs_stage.at[k, row], rhs_sem, k, step, (layer, to, col))
+
+    def inv_copy(k, step):
+        return remote(inverses[k], inv_stage.at[k, row], inv_sem, k, step, (layer, ahead(row, step), col))
+
+    def rhs_z_copy(k, step):
+        to = ahead(col, step)
+        return remote(rhs_stage.at[k, to], rhs_full.at[k, col], rhs_z_sem, k, step, (layer, row, to))
+
+    def inv_z_copy(k, step):
+        to = ahead(col, step)
+        return remote(inv_stage.at[k, to], inv_full.at[k, col], inv_z_sem, k, step, (layer, row, to))
+
+    def part_copy(k, step):
+        to = ahead(col, step)
+        return remote(part.at[k, to], arrived.at[k, col], part_sem, k, step, (layer, row, to))
+
+    def cross_copy(step):
+        return remote(
+            cross.at[0], cross.at[step], cross_sem, 0, step, (ahead(layer, step, layers), row, col)
+        )
+
+    rows = width // grid
+
+    def out_z_copy(k, step):
+        to = ahead(col, step)
+        return remote(solved.at[k, to], out_stage.at[k, col], out_z_sem, k, step, (layer, row, to))
+
+    def out_copy(k, step):
+        to = ahead(row, step)
+        return remote(out_stage.at[k, to], out_full.at[k, row], out_sem, k, step, (layer, to, col))
+
+    sent = []
+
+    def start(make, k):
+        for step in others:
+            copy = make(k, step)
+            copy.start()
+            sent.append(copy)
+
+    def arrive(make, k):
+        for step in others:
+            make(k, step).wait_recv()
+
+    def spread_coupling(k):
+        mask(k)
+        start(coupling_copy, k)
+
+    def rhs_row(k):
+        start(rhs_copy, k)
+        rhs_stage[k, row] = rhs_split[k, row]
+
+    def inv_row(k):
+        start(inv_copy, k)
+        inv_stage[k, row] = inverses[k][...]
+
+    def rhs_col(k):
+        arrive(rhs_copy, k)
+        start(rhs_z_copy, k)
+        rhs_full[k, col] = rhs_stage[k, col]
+
+    def inv_col(k):
+        arrive(inv_copy, k)
+        start(inv_z_copy, k)
+        inv_full[k, col] = inv_stage[k, col]
+
+    def split(k):
+        for piece in range(grid):
+            rhs_split[k, piece] = rights[k][:, piece * columns : (piece + 1) * columns]
+
+    def right_side(k):
+        arrive(rhs_z_copy, k)
+        return rhs_full[k].reshape(width, columns)
+
+    def apply_inverse(k, value):
+        arrive(inv_z_copy, k)
+        return dot(inv_full[k].reshape(width, width), value)
+
+    def couple(level, k, value, first, send):
+        arrive(coupling_copy, k)
+
+        def body(at, carry):
+            to = lax.rem(col + 1 + at, grid)
+            product = dot(coupling[k, to], value)
+            if not first:
+                product = part[level, to] + product
+            part[level, to] = product
+            return carry
+
+        if not send:
+            lax.fori_loop(0, grid, body, 0)
+            return
+
+        def body_send(at, carry):
+            body(at, carry)
+            part_copy(level, at + 1).start()
+            return carry
+
+        lax.fori_loop(0, grid - 1, body_send, 0)
+        body(grid - 1, 0)
+        sent.extend(part_copy(level, step) for step in others)
+
+    def reduced(level):
+        total = part[level, col]
+        for step in others:
+            part_copy(level, step).wait_recv()
+            total = total + arrived[level, lax.rem(col + grid - step, grid)]
+        return total
+
+    def emit(k, value):
+        solved[k] = value.reshape(grid, rows, columns)
+        start(out_z_copy, k)
+        out_stage[k, col] = solved[k, col]
+
+    def emit_row(k):
+        arrive(out_z_copy, k)
+        start(out_copy, k)
+        out_full[k, row] = out_stage[k, row]
+
+    split(0)
+    mask(0)
+    pl.semaphore_wait(barrier, 2 * (grid - 1) + layers - 1)
+    rhs_row(0)
+    inv_row(0)
+    start(coupling_copy, 0)
+    split(1)
+    split(2)
+    split(3)
+    rhs_row(1)
+    inv_row(1)
+    rhs_col(0)
+    inv_col(0)
+    spread_coupling(1)
+    spread_coupling(2)
+    rhs_row(2)
+    inv_row(2)
+    rhs_row(3)
+    inv_row(3)
+    rhs_zero = right_side(0)
+    rhs_col(1)
+    inv_col(1)
+    fore_zero = apply_inverse(0, rhs_zero)
+    couple(0, 0, fore_zero, True, True)
+    spread_coupling(3)
+    spread_coupling(4)
+    couple(1, 1, fore_zero, True, False)
+    rhs_one = right_side(1)
+    total = reduced(0)
+    rhs_col(2)
+    inv_col(2)
+    fore_one = apply_inverse(1, rhs_one - total)
+    couple(1, 2, fore_one, False, True)
+    spread_coupling(5)
+    spread_coupling(6)
+    inv_row(7)
+    inv_row(6)
+    couple(2, 3, fore_zero, True, False)
+    couple(2, 4, fore_one, False, False)
+    rhs_two = right_side(2)
+    total = reduced(1)
+    rhs_col(3)
+    inv_col(3)
+    fore_two = apply_inverse(2, rhs_two - total)
+    couple(2, 5, fore_two, False, True)
+    spread_coupling(7)
+    spread_coupling(8)
+    inv_row(5)
+    inv_row(4)
+    inv_col(7)
+    inv_col(6)
+    spread_coupling(9)
+    spread_coupling(10)
+    spread_coupling(11)
+    rhs_last = right_side(3)
+    cross[0] = reduced(2)
+    for step in range(1, layers):
+        cross_copy(step).start()
+    total = cross[0]
+    for step in range(1, layers):
+        cross_copy(step).wait_recv()
+        total = total + cross[step]
+    final_top = apply_inverse(7, apply_inverse(3, rhs_last - total))
+    couple(3, 6, final_top, True, True)
+    emit(3, final_top)
+    couple(4, 7, final_top, True, False)
+    residual = fore_two - reduced(3)
+    inv_col(5)
+    final_two = apply_inverse(6, residual)
+    couple(4, 8, final_two, False, True)
+    emit(2, final_two)
+    emit_row(3)
+    couple(5, 9, final_top, True, False)
+    couple(5, 10, final_two, False, False)
+    residual = fore_one - reduced(4)
+    inv_col(4)
+    final_one = apply_inverse(5, residual)
+    couple(5, 11, final_one, False, True)
+    emit(1, final_one)
+    emit_row(2)
+    final_zero = apply_inverse(4, fore_zero - reduced(5))
+    emit(0, final_zero)
+    emit_row(1)
+    emit_row(0)
+
+    for k in (3, 2, 1, 0):
+        arrive(out_copy, k)
+        for piece in range(grid):
+            target = out_top if k == LEVELS else out_sub.at[k]
+            target[:, piece * columns : (piece + 1) * columns] = out_full[k, piece]
+    for copy in sent:
+        copy.wait_send()
+    for step in range(1, layers):
+        cross_copy(step).wait_send()
+
+
+def solve_in_kernel(
+    layers,
+    grid,
+    rhs_sub,
+    rhs_top,
+    lower_inv_sub,
+    lower_inv_top,
+    upper_inv_sub,
+    upper_inv_top,
+    lower_sub,
+    lower_top,
+    upper_sub,
+    upper_top,
+    block_pattern,
+):
+    rows, count = rhs_top.shape[-2:]
+    width = lower_inv_top.shape[-1]
+    columns = count // grid
+    levels = LEVELS + 1
+    steps = 2 * LEVELS
+    couplings = 4 * LEVELS
+    f32 = jnp.float32
+
+    def sub(array):
+        return array.reshape((LEVELS,) + array.shape[-2:])
+
+    def top(array):
+        return array.reshape(array.shape[-2:])
+
+    def sems(number, peers=grid):
+        return pltpu.SemaphoreType.DMA((2, number, peers - 1))
+
+    vmem = pl.BlockSpec(memory_space=pltpu.VMEM)
+    out_sub, out_top = pl.pallas_call(
+        functools.partial(kernel, layers, grid),
+        out_shape=(
+            jax.ShapeDtypeStruct((LEVELS, rows, count), f32),
+            jax.ShapeDtypeStruct((rows, count), f32),
+        ),
+        in_specs=[pl.BlockSpec(memory_space=pltpu.SMEM)] + [vmem] * 10,
+        out_specs=(vmem, vmem),
+        scratch_shapes=[
+            pltpu.VMEM((couplings, grid, width, width), f32),
+            pltpu.VMEM((levels, grid, rows, columns), f32),
+            pltpu.VMEM((levels, grid, rows, columns), f32),
+            pltpu.VMEM((levels, grid, rows, columns), f32),
+            pltpu.VMEM((2 * levels, grid, rows, width), f32),
+            pltpu.VMEM((2 * levels, grid, rows, width), f32),
+            pltpu.VMEM((steps, grid, width, columns), f32),
+            pltpu.VMEM((steps, grid, width, columns), f32),
+            pltpu.VMEM((levels, grid, rows, columns), f32),
+            pltpu.VMEM((layers, width, columns), f32),
+            pltpu.VMEM((levels, grid, rows, columns), f32),
+            pltpu.VMEM((levels, grid, rows, columns), f32),
+            sems(couplings),
+            sems(levels),
+            sems(levels),
+            sems(2 * levels),
+            sems(2 * levels),
+            sems(steps),
+            sems(1, layers),
+            sems(levels),
+            sems(levels),
+        ],
+        compiler_params=pltpu.CompilerParams(
+            collective_id=0, has_side_effects=True, vmem_limit_bytes=48 * 2**20
+        ),
+        cost_estimate=pl.CostEstimate(
+            flops=2 * couplings * grid * width * width * columns,
+            bytes_accessed=4 * couplings * width * width,
+            transcendentals=0,
+        ),
+    )(
+        block_pattern.reshape(-1),
+        sub(rhs_sub),
+        top(rhs_top),
+        sub(lower_inv_sub),
+        top(lower_inv_top),
+        sub(upper_inv_sub),
+        top(upper_inv_top),
+        sub(lower_sub),
+        sub(lower_top),
+        sub(upper_sub),
+        sub(upper_top),
+    )
+    return out_sub.reshape(rhs_sub.shape), out_top.reshape(rhs_top.shape)
 
 
 def broadcast(x, axis, root):
@@ -115,8 +521,19 @@
         P("layer", None, None, "row", None, "col", None, None),
         P("layer", None, None, None, "row", None, "col"),
     )
+    layers, grid = mesh.shape["layer"], mesh.shape["row"]
+
+    def choose(*arguments):
+        rhs_sub, rhs_top, inverse = arguments[0], arguments[1], arguments[3]
+        columns, width = rhs_top.shape[-1] // grid, inverse.shape[-1]
+        square = mesh.shape["row"] == mesh.shape["col"] and rhs_sub.shape[2] == 1
+        held = 4 * 4 * LEVELS * grid * width * width
+        if square and grid > 1 and rhs_top.shape[-1] % (128 * grid) == 0 and held <= 2**24:
+            return solve_in_kernel(layers, grid, *arguments)
+        return on_device(*arguments)
+
     return jax.shard_map(
-        on_device,
+        choose,
         mesh=mesh,
         in_specs=placed,
         out_specs=(P("layer", None, None, "row", "col", None), P(None, "row", "col", None)),

time: 629 us -> 211 us (0.34)
  waiting for transfers between devices: 450 us -> 0 us
  Pallas kernels: 0 us -> 197 us
  blocking collectives: 101 us -> 0 us
  matrix products: 38.7 us -> 0 us
  between operations: 21.7 us -> 0.66 us
    psum x12 -> x0, waiting for transfers between devices: 431 us -> none  [the longest x6 257 us: broadcast(): return lax.psum(jnp.where(mine, x, jnp.zeros_like(x)), axis)]
    pallas_call x0 -> x1, Pallas kernels: none -> 197 us  [solve_in_kernel(): pl.pallas_call(functools.partial(kernel, layers, grid), out_shape=(jax.Sh...]
    all_gather x5 -> x0, blocking collectives: 101 us -> none  [the longest x1 27.4 us: on_device(): lax.all_gather(upper_inv_sub, 'col', axis=4, tiled=True)]
    dot_general x20 -> x0, matrix products: 38.7 us -> none  [the longest x12 27.3 us: couple(): return jnp.einsum('tsab,tsbn->tan', blocks, weighted, precision=HIGHEST)]
    all_gather x1 -> x0, waiting for transfers between devices: 18.7 us -> none  [on_device(): lax.all_gather(rhs_sub, 'col', axis=4, tiled=True)]
    unnamed x22 -> x25, local copies, waits for them, and re-layouts: 4.84 us -> 12.1 us
  transfers between devices with their start and end apart: 13 -> 0, of which waited for: 13 -> 0; matrix products, arithmetic and copies ran while one was open for 2% -> 0% of each run, Pallas kernels for 0% -> 0%
where the time goes in v1:
time: 211 us; the launch traced here: 210 us
  Pallas kernels  197 us (93%)
  local copies, waits for them, and re-layouts  12.2 us (6%)
    pallas_call x1, Pallas kernels, solve_in_kernel(): pl.pallas_call(functools.partial(kernel, layers, grid), out_shape=(jax.Sh...  197 us
    unnamed x25, local copies, waits for them, and re-layouts  12.1 us

profile of v1, /device:TPU:0, one launch (start us, length us, event | category | flops | bytes accessed | tf_op | source)
XLA Modules:
  0.0 210.2 jit_solution(13986707365912319612)
XLA Ops:
  0.6 0.0 copy-start.10
  0.6 0.7 copy-done.10
  1.3 0.1 copy.15
  1.4 0.1 reshape.43.pattern
  1.5 0.0 copy-start
  1.5 1.1 copy-done
  2.6 0.0 copy-start.1
  2.6 1.1 copy-done.1
  3.8 0.0 copy-start.2
  3.8 1.1 copy-done.2
  4.9 0.0 copy-start.3
  4.9 1.1 copy-done.3
  6.0 0.0 copy-start.4
  6.0 1.0 copy-done.4
  7.0 0.0 copy-start.5
  7.0 0.9 copy-done.5
  7.9 0.0 copy-start.6
  8.0 0.9 copy-done.6
  8.9 0.0 copy-start.7
  8.9 0.9 copy-done.7
  9.8 0.0 copy-start.8
  9.8 0.8 copy-done.8
  10.6 0.0 copy-start.9
  10.6 0.8 copy-done.9
  11.5 197.3 %shard_map.122 = (f32[3,64,512]{2,1,0:T(8,128)S(1)}, f32[64,512]{1,0:T(8,128)S(1)}) custom-call(s32[12]{0:T(128)S(1)} %reshape.43.pattern, f32[3,64,512]{2,1,0:T(8,128)S(1)} %bitcast.20, f32[64,512]{1,0:T(8,128)S(1)} %bitcast.24, f32[3,64,256]{2,1,0:T(8,128)S(1)} %bitcast.22, f32[64,256]{1,0:T(8,128)S(1)} %bitcast.26, f32[3,64,256]{2,1,0:T(8,128)S(1)} %bitcast.23, ...), custom_call_target="tpu_custom_call" | custom-call | flops 805306368 | bytes 3145728 | tf_op jit(solution)/shard_map/pallas_call | solution.py:360
  208.8 0.7 copy.19
  209.5 0.7 copy.20
Async XLA Ops:
  0.6 0.7 copy-start.10
  1.5 1.1 copy-start
  2.6 1.1 copy-start.1
  3.8 1.1 copy-start.2
  4.9 1.1 copy-start.3
  6.0 1.0 copy-start.4
  7.0 0.9 copy-start.5
  7.9 0.9 copy-start.6
  8.9 0.9 copy-start.7
  9.8 0.8 copy-start.8
  10.6 0.8 copy-start.9

commit v2 on v1

--- a/solution.py
+++ b/solution.py
@@ -11,8 +11,21 @@
 LEVELS = 3
 
 
-def dot(a, b):
-    return jnp.dot(a, b, precision=HIGHEST, preferred_element_type=jnp.float32)
+def halves(value):
+    high = value.astype(jnp.bfloat16)
+    return high, (value - high.astype(jnp.float32)).astype(jnp.bfloat16)
+
+
+def pair(value):
+    return jnp.concatenate(halves(value), axis=1)
+
+
+def dot(a, paired):
+    high, low = halves(a)
+    both = jnp.dot(high, paired, preferred_element_type=jnp.float32)
+    both = both + jnp.dot(low, paired, preferred_element_type=jnp.float32)
+    columns = paired.shape[1] // 2
+    return both[:, :columns] + both[:, columns:]
 
 
 def kernel(
@@ -31,6 +44,8 @@
     upper_top,
     out_sub,
     out_top,
+    own,
+    own_rhs,
     coupling,
     rhs_split,
     rhs_stage,
@@ -43,6 +58,9 @@
     cross,
     out_stage,
     out_full,
+    own_sem,
+    own_rhs_sem,
+    own_inv_sem,
     coupling_sem,
     rhs_sem,
     rhs_z_sem,
@@ -98,21 +116,59 @@
     inverses += tuple(upper_inv_sub.at[k] for k in range(LEVELS)) + (upper_inv_top,)
     rights = tuple(rhs_sub.at[k] for k in range(LEVELS)) + (rhs_top,)
 
+    def own_copy(k):
+        ref, at, _ = sources[k]
+        return pltpu.make_async_copy(ref.at[at], own.at[k], own_sem.at[k])
+
+    def own_rhs_copy(k):
+        return pltpu.make_async_copy(rights[k], own_rhs.at[k], own_rhs_sem.at[k])
+
+    def own_inv_copy(k):
+        return pltpu.make_async_copy(inverses[k], inv_stage.at[k, row], own_inv_sem.at[k])
+
+    own_rhs_copy(0).start()
+    own_inv_copy(0).start()
+    own_copy(0).start()
+    for k in range(1, LEVELS + 1):
+        own_rhs_copy(k).start()
+        own_inv_copy(k).start()
+    for k in range(1, len(sources)):
+        own_copy(k).start()
+    for k in range(LEVELS + 1, len(inverses)):
+        own_inv_copy(k).start()
+
     def mask(k):
-        ref, pair, kind = sources[k]
-        coupling[k, row] = ref[pair] * pattern[kind * LEVELS + pair].astype(jnp.float32)
+        _, at, kind = sources[k]
+        own_copy(k).wait()
+        coupling[k, row] = own[k] * pattern[kind * LEVELS + at].astype(jnp.float32)
+
+    half = grid // 2
+    beside = row + 1 - 2 * lax.rem(row, 2)
+    above = lax.rem(row + half, grid)
+    upper, lower = pl.ds(0, width // 2), pl.ds(width // 2, width // 2)
 
     def coupling_copy(k, step):
-        return remote(
-            coupling.at[k, row], coupling.at[k, row], coupling_sem, k, step, (layer, ahead(row, step), col)
-        )
+        to = (beside, above)[step - 1]
+        return remote(coupling.at[k, row], coupling.at[k, row], coupling_sem, k, step, (layer, to, col))
+
+    def relay_copy(k, step):
+        come, to, part_rows = ((beside, above, upper), (above, beside, lower))[step - 1]
+        block = coupling.at[k, come, part_rows]
+        return remote(block, block, coupling_sem, k, step + 2, (layer, to, col))
+
+    def relay(k):
+        for step in (1, 2):
+            coupling_copy(k, step).wait_recv()
+            copy = relay_copy(k, step)
+            copy.start()
+            sent.append(copy)
 
     def rhs_copy(k, step):
         to = ahead(row, step)
         return remote(rhs_split.at[k, to], rhs_stage.at[k, row], rhs_sem, k, step, (layer, to, col))
 
     def inv_copy(k, step):
-        return remote(inverses[k], inv_stage.at[k, row], inv_sem, k, step, (layer, ahead(row, step), col))
+        return remote(inv_stage.at[k, row], inv_stage.at[k, row], inv_sem, k, step, (layer, ahead(row, step), col))
 
     def rhs_z_copy(k, step):
         to = ahead(col, step)
@@ -155,15 +211,18 @@
 
     def spread_coupling(k):
         mask(k)
-        start(coupling_copy, k)
+        for step in (1, 2):
+            copy = coupling_copy(k, step)
+            copy.start()
+            sent.append(copy)
 
     def rhs_row(k):
         start(rhs_copy, k)
         rhs_stage[k, row] = rhs_split[k, row]
 
     def inv_row(k):
+        own_inv_copy(k).wait()
         start(inv_copy, k)
-        inv_stage[k, row] = inverses[k][...]
 
     def rhs_col(k):
         arrive(rhs_copy, k)
@@ -176,8 +235,9 @@
         inv_full[k, col] = inv_stage[k, col]
 
     def split(k):
+        own_rhs_copy(k).wait()
         for piece in range(grid):
-            rhs_split[k, piece] = rights[k][:, piece * columns : (piece + 1) * columns]
+            rhs_split[k, piece] = own_rhs[k, :, piece * columns : (piece + 1) * columns]
 
     def right_side(k):
         arrive(rhs_z_copy, k)
@@ -185,10 +245,11 @@
 
     def apply_inverse(k, value):
         arrive(inv_z_copy, k)
-        return dot(inv_full[k].reshape(width, width), value)
+        return dot(inv_full[k].reshape(width, width), pair(value))
 
     def couple(level, k, value, first, send):
-        arrive(coupling_copy, k)
+        for step in (1, 2):
+            relay_copy(k, step).wait_recv()
 
         def body(at, carry):
             to = lax.rem(col + 1 + at, grid)
@@ -228,60 +289,64 @@
         start(out_copy, k)
         out_full[k, row] = out_stage[k, row]
 
+    pl.semaphore_wait(barrier, 2 * (grid - 1) + layers - 1)
     split(0)
-    mask(0)
-    pl.semaphore_wait(barrier, 2 * (grid - 1) + layers - 1)
     rhs_row(0)
     inv_row(0)
-    start(coupling_copy, 0)
-    split(1)
-    split(2)
-    split(3)
+    spread_coupling(0)
+    for k in range(1, LEVELS + 1):
+        split(k)
     rhs_row(1)
     inv_row(1)
+    spread_coupling(1)
     rhs_col(0)
     inv_col(0)
-    spread_coupling(1)
     spread_coupling(2)
+    relay(0)
+    rhs_col(1)
+    inv_col(1)
     rhs_row(2)
     inv_row(2)
+    spread_coupling(3)
+    fore_zero = apply_inverse(0, right_side(0))
+    fore_zero_pair = pair(fore_zero)
+    couple(0, 0, fore_zero_pair, True, True)
+    relay(1)
+    spread_coupling(4)
+    relay(2)
+    spread_coupling(5)
     rhs_row(3)
     inv_row(3)
-    rhs_zero = right_side(0)
-    rhs_col(1)
-    inv_col(1)
-    fore_zero = apply_inverse(0, rhs_zero)
-    couple(0, 0, fore_zero, True, True)
-    spread_coupling(3)
-    spread_coupling(4)
-    couple(1, 1, fore_zero, True, False)
-    rhs_one = right_side(1)
+    couple(1, 1, fore_zero_pair, True, False)
     total = reduced(0)
     rhs_col(2)
     inv_col(2)
-    fore_one = apply_inverse(1, rhs_one - total)
-    couple(1, 2, fore_one, False, True)
-    spread_coupling(5)
+    fore_one = apply_inverse(1, right_side(1) - total)
+    fore_one_pair = pair(fore_one)
+    couple(1, 2, fore_one_pair, False, True)
+    relay(3)
     spread_coupling(6)
     inv_row(7)
     inv_row(6)
-    couple(2, 3, fore_zero, True, False)
-    couple(2, 4, fore_one, False, False)
-    rhs_two = right_side(2)
-    total = reduced(1)
+    relay(4)
+    spread_coupling(7)
+    couple(2, 3, fore_zero_pair, True, False)
     rhs_col(3)
     inv_col(3)
-    fore_two = apply_inverse(2, rhs_two - total)
-    couple(2, 5, fore_two, False, True)
-    spread_coupling(7)
+    couple(2, 4, fore_one_pair, False, False)
+    total = reduced(1)
+    relay(5)
+    fore_two = apply_inverse(2, right_side(2) - total)
     spread_coupling(8)
+    couple(2, 5, pair(fore_two), False, True)
+    relay(6)
+    spread_coupling(9)
     inv_row(5)
     inv_row(4)
     inv_col(7)
     inv_col(6)
-    spread_coupling(9)
+    relay(7)
     spread_coupling(10)
-    spread_coupling(11)
     rhs_last = right_side(3)
     cross[0] = reduced(2)
     for step in range(1, layers):
@@ -291,21 +356,28 @@
         cross_copy(step).wait_recv()
         total = total + cross[step]
     final_top = apply_inverse(7, apply_inverse(3, rhs_last - total))
-    couple(3, 6, final_top, True, True)
+    final_top_pair = pair(final_top)
+    couple(3, 6, final_top_pair, True, True)
     emit(3, final_top)
-    couple(4, 7, final_top, True, False)
+    relay(8)
+    spread_coupling(11)
+    couple(4, 7, final_top_pair, True, False)
+    relay(9)
     residual = fore_two - reduced(3)
     inv_col(5)
     final_two = apply_inverse(6, residual)
-    couple(4, 8, final_two, False, True)
+    final_two_pair = pair(final_two)
+    couple(4, 8, final_two_pair, False, True)
     emit(2, final_two)
     emit_row(3)
-    couple(5, 9, final_top, True, False)
-    couple(5, 10, final_two, False, False)
+    relay(10)
+    couple(5, 9, final_top_pair, True, False)
+    relay(11)
+    couple(5, 10, final_two_pair, False, False)
     residual = fore_one - reduced(4)
     inv_col(4)
     final_one = apply_inverse(5, residual)
-    couple(5, 11, final_one, False, True)
+    couple(5, 11, pair(final_one), False, True)
     emit(1, final_one)
     emit_row(2)
     final_zero = apply_inverse(4, fore_zero - reduced(5))
@@ -363,9 +435,11 @@
             jax.ShapeDtypeStruct((LEVELS, rows, count), f32),
             jax.ShapeDtypeStruct((rows, count), f32),
         ),
-        in_specs=[pl.BlockSpec(memory_space=pltpu.SMEM)] + [vmem] * 10,
+        in_specs=[pl.BlockSpec(memory_space=pltpu.SMEM)] + [pl.BlockSpec(memory_space=pl.ANY)] * 10,
         out_specs=(vmem, vmem),
         scratch_shapes=[
+            pltpu.VMEM((couplings, width, width), f32),
+            pltpu.VMEM((levels, rows, count), f32),
             pltpu.VMEM((couplings, grid, width, width), f32),
             pltpu.VMEM((levels, grid, rows, columns), f32),
             pltpu.VMEM((levels, grid, rows, columns), f32),
@@ -378,7 +452,10 @@
             pltpu.VMEM((layers, width, columns), f32),
             pltpu.VMEM((levels, grid, rows, columns), f32),
             pltpu.VMEM((levels, grid, rows, columns), f32),
-            sems(couplings),
+            pltpu.SemaphoreType.DMA((couplings,)),
+            pltpu.SemaphoreType.DMA((levels,)),
+            pltpu.SemaphoreType.DMA((2 * levels,)),
+            pltpu.SemaphoreType.DMA((2, couplings, 4)),
             sems(levels),
             sems(levels),
             sems(2 * levels),
@@ -528,7 +605,7 @@
         columns, width = rhs_top.shape[-1] // grid, inverse.shape[-1]
         square = mesh.shape["row"] == mesh.shape["col"] and rhs_sub.shape[2] == 1
         held = 4 * 4 * LEVELS * grid * width * width
-        if square and grid > 1 and rhs_top.shape[-1] % (128 * grid) == 0 and held <= 2**24:
+        if square and grid == 4 and rhs_top.shape[-1] % (128 * grid) == 0 and held <= 2**24:
             return solve_in_kernel(layers, grid, *arguments)
         return on_device(*arguments)
 

time: 211 us -> 194 us (0.919)
  Pallas kernels: 197 us -> 181 us
    pallas_call x1, Pallas kernels: 197 us -> 181 us  [solve_in_kernel(): pl.pallas_call(functools.partial(kernel, layers, grid), out_shape=(jax.Sh...]
where the time goes in v2:
time: 194 us; the launch traced here: 193 us
  Pallas kernels  181 us (93%)
  local copies, waits for them, and re-layouts  12.2 us (6%)
    pallas_call x1, Pallas kernels, solve_in_kernel(): pl.pallas_call(functools.partial(kernel, layers, grid), out_shape=(jax.Sh...  181 us
    unnamed x25, local copies, waits for them, and re-layouts  12.1 us

profile of v2, /device:TPU:0, one launch (start us, length us, event | category | flops | bytes accessed | tf_op | source)
XLA Modules:
  0.0 193.4 jit_solution(14277415490439003820)
XLA Ops:
  0.6 0.0 copy-start.10
  0.6 0.7 copy-done.10
  1.3 0.1 copy.15
  1.4 0.1 reshape.43.pattern
  1.5 0.0 copy-start
  1.5 1.1 copy-done
  2.6 0.0 copy-start.1
  2.6 1.1 copy-done.1
  3.8 0.0 copy-start.2
  3.8 1.1 copy-done.2
  4.9 0.0 copy-start.3
  4.9 1.1 copy-done.3
  6.0 0.0 copy-start.4
  6.0 1.0 copy-done.4
  7.0 0.0 copy-start.5
  7.0 0.9 copy-done.5
  7.9 0.0 copy-start.6
  8.0 0.9 copy-done.6
  8.9 0.0 copy-start.7
  8.9 0.9 copy-done.7
  9.8 0.0 copy-start.8
  9.8 0.8 copy-done.8
  10.6 0.0 copy-start.9
  10.6 0.8 copy-done.9
  11.5 180.5 %shard_map.122 = (f32[3,64,512]{2,1,0:T(8,128)S(1)}, f32[64,512]{1,0:T(8,128)S(1)}) custom-call(s32[12]{0:T(128)S(1)} %reshape.43.pattern, f32[3,64,512]{2,1,0:T(8,128)S(1)} %bitcast.20, f32[64,512]{1,0:T(8,128)S(1)} %bitcast.24, f32[3,64,256]{2,1,0:T(8,128)S(1)} %bitcast.22, f32[64,256]{1,0:T(8,128)S(1)} %bitcast.26, f32[3,64,256]{2,1,0:T(8,128)S(1)} %bitcast.23, ...), custom_call_target="tpu_custom_call" | custom-call | flops 805306368 | bytes 3145728 | tf_op jit(solution)/shard_map/pallas_call | solution.py:432
  192.0 0.7 copy.19
  192.7 0.7 copy.20
Async XLA Ops:
  0.6 0.7 copy-start.10
  1.5 1.1 copy-start
  2.6 1.1 copy-start.1
  3.8 1.1 copy-start.2
  4.9 1.1 copy-start.3
  6.0 1.0 copy-start.4
  7.0 0.9 copy-start.5
  7.9 0.9 copy-start.6
  8.9 0.9 copy-start.7
  9.8 0.8 copy-start.8
  10.6 0.8 copy-start.9

commit v3 on v2

--- a/solution.py
+++ b/solution.py
@@ -53,6 +53,7 @@
     inv_stage,
     inv_full,
     part,
+    given,
     arrived,
     solved,
     cross,
@@ -178,9 +179,17 @@
         to = ahead(col, step)
         return remote(inv_stage.at[k, to], inv_full.at[k, col], inv_z_sem, k, step, (layer, row, to))
 
-    def part_copy(k, step):
-        to = ahead(col, step)
-        return remote(part.at[k, to], arrived.at[k, col], part_sem, k, step, (layer, row, to))
+    mate = col + 1 - 2 * lax.rem(col, 2)
+    keep, give = lax.rem(col + half, grid), lax.rem(mate + half, grid)
+
+    def give_copy(k):
+        return remote(part.at[k, give], given.at[k], part_sem, k, 1, (layer, row, mate))
+
+    def near_copy(k):
+        return remote(part.at[k, mate], arrived.at[k, 0], part_sem, k, 2, (layer, row, mate))
+
+    def far_copy(k):
+        return remote(part.at[k, keep], arrived.at[k, 1], part_sem, k, 3, (layer, row, keep))
 
     def cross_copy(step):
         return remote(
@@ -251,33 +260,37 @@
         for step in (1, 2):
             relay_copy(k, step).wait_recv()
 
-        def body(at, carry):
-            to = lax.rem(col + 1 + at, grid)
+        def add(to):
             product = dot(coupling[k, to], value)
             if not first:
                 product = part[level, to] + product
             part[level, to] = product
-            return carry
 
         if not send:
+
+            def body(to, carry):
+                add(to)
+                return carry
+
             lax.fori_loop(0, grid, body, 0)
             return
 
-        def body_send(at, carry):
-            body(at, carry)
-            part_copy(level, at + 1).start()
-            return carry
-
-        lax.fori_loop(0, grid - 1, body_send, 0)
-        body(grid - 1, 0)
-        sent.extend(part_copy(level, step) for step in others)
+        add(give)
+        give_copy(level).start()
+        add(mate)
+        near_copy(level).start()
+        add(keep)
+        give_copy(level).wait_recv()
+        part[level, keep] = part[level, keep] + given[level]
+        far_copy(level).start()
+        add(col)
+        sent.extend((give_copy(level), near_copy(level), far_copy(level)))
 
     def reduced(level):
-        total = part[level, col]
-        for step in others:
-            part_copy(level, step).wait_recv()
-            total = total + arrived[level, lax.rem(col + grid - step, grid)]
-        return total
+        near_copy(level).wait_recv()
+        total = part[level, col] + arrived[level, 0]
+        far_copy(level).wait_recv()
+        return total + arrived[level, 1]
 
     def emit(k, value):
         solved[k] = value.reshape(grid, rows, columns)
@@ -435,7 +448,7 @@
             jax.ShapeDtypeStruct((LEVELS, rows, count), f32),
             jax.ShapeDtypeStruct((rows, count), f32),
         ),
-        in_specs=[pl.BlockSpec(memory_space=pltpu.SMEM)] + [pl.BlockSpec(memory_space=pl.ANY)] * 10,
+        in_specs=[pl.BlockSpec(memory_space=pltpu.SMEM)] + [pl.BlockSpec(memory_space=pltpu.HBM)] * 10,
         out_specs=(vmem, vmem),
         scratch_shapes=[
             pltpu.VMEM((couplings, width, width), f32),
@@ -447,7 +460,8 @@
             pltpu.VMEM((2 * levels, grid, rows, width), f32),
             pltpu.VMEM((2 * levels, grid, rows, width), f32),
             pltpu.VMEM((steps, grid, width, columns), f32),
-            pltpu.VMEM((steps, grid, width, columns), f32),
+            pltpu.VMEM((steps, width, columns), f32),
+            pltpu.VMEM((steps, 2, width, columns), f32),
             pltpu.VMEM((levels, grid, rows, columns), f32),
             pltpu.VMEM((layers, width, columns), f32),
             pltpu.VMEM((levels, grid, rows, columns), f32),

time: 194 us -> 187 us (0.964)
  Pallas kernels: 181 us -> 173 us
    pallas_call x1, Pallas kernels: 181 us -> 173 us  [solve_in_kernel(): pl.pallas_call(functools.partial(kernel, layers, grid), out_shape=(jax.Sh...]
where the time goes in v3:
time: 187 us; the launch traced here: 186 us
  Pallas kernels  173 us (93%)
  local copies, waits for them, and re-layouts  12.2 us (7%)
    pallas_call x1, Pallas kernels, solve_in_kernel(): pl.pallas_call(functools.partial(kernel, layers, grid), out_shape=(jax.Sh...  173 us
    unnamed x25, local copies, waits for them, and re-layouts  12.1 us

profile of v3, /device:TPU:0, one launch (start us, length us, event | category | flops | bytes accessed | tf_op | source)
XLA Modules:
  0.0 186.1 jit_solution(15510167837150263286)
XLA Ops:
  0.6 0.0 copy-start.10
  0.6 0.7 copy-done.10
  1.3 0.1 copy.15
  1.4 0.1 reshape.43.pattern
  1.5 0.0 copy-start
  1.5 1.1 copy-done
  2.6 0.0 copy-start.1
  2.6 1.1 copy-done.1
  3.8 0.0 copy-start.2
  3.8 1.1 copy-done.2
  4.9 0.0 copy-start.3
  4.9 1.1 copy-done.3
  6.0 0.0 copy-start.4
  6.0 1.0 copy-done.4
  7.0 0.0 copy-start.5
  7.0 0.9 copy-done.5
  7.9 0.0 copy-start.6
  8.0 0.9 copy-done.6
  8.9 0.0 copy-start.7
  8.9 0.9 copy-done.7
  9.8 0.0 copy-start.8
  9.8 0.8 copy-done.8
  10.6 0.0 copy-start.9
  10.6 0.8 copy-done.9
  11.5 173.2 %shard_map.122 = (f32[3,64,512]{2,1,0:T(8,128)S(1)}, f32[64,512]{1,0:T(8,128)S(1)}) custom-call(s32[12]{0:T(128)S(1)} %reshape.43.pattern, f32[3,64,512]{2,1,0:T(8,128)S(1)} %bitcast.20, f32[64,512]{1,0:T(8,128)S(1)} %bitcast.24, f32[3,64,256]{2,1,0:T(8,128)S(1)} %bitcast.22, f32[64,256]{1,0:T(8,128)S(1)} %bitcast.26, f32[3,64,256]{2,1,0:T(8,128)S(1)} %bitcast.23, ...), custom_call_target="tpu_custom_call" | custom-call | flops 805306368 | bytes 3145728 | tf_op jit(solution)/shard_map/pallas_call | solution.py:445
  184.7 0.7 copy.19
  185.4 0.7 copy.20
Async XLA Ops:
  0.6 0.7 copy-start.10
  1.5 1.1 copy-start
  2.6 1.1 copy-start.1
  3.8 1.1 copy-start.2
  4.9 1.1 copy-start.3
  6.0 1.0 copy-start.4
  7.0 0.9 copy-start.5
  7.9 0.9 copy-start.6
  8.9 0.9 copy-start.7
  9.8 0.8 copy-start.8
  10.6 0.8 copy-start.9

commit v4 on v3

--- a/solution.py
+++ b/solution.py
@@ -67,6 +67,7 @@
     rhs_z_sem,
     inv_sem,
     inv_z_sem,
+    share_sem,
     part_sem,
     cross_sem,
     out_z_sem,
@@ -168,8 +169,22 @@
         to = ahead(row, step)
         return remote(rhs_split.at[k, to], rhs_stage.at[k, row], rhs_sem, k, step, (layer, to, col))
 
+    rows = width // grid
+    share = rows // layers
+
+    def inv_rows(k):
+        return (layer * share, share) if k % (LEVELS + 1) == LEVELS else (0, rows)
+
     def inv_copy(k, step):
-        return remote(inv_stage.at[k, row], inv_stage.at[k, row], inv_sem, k, step, (layer, ahead(row, step), col))
+        to = (beside, above)[step - 1]
+        block = inv_stage.at[k, row, pl.ds(*inv_rows(k))]
+        return remote(block, block, inv_sem, k, step, (layer, to, col))
+
+    def inv_relay_copy(k, step):
+        come, to, second = ((beside, above, 0), (above, beside, 1))[step - 1]
+        first, count = inv_rows(k)
+        block = inv_stage.at[k, come, pl.ds(first + second * (count // 2), count // 2)]
+        return remote(block, block, inv_sem, k, step + 2, (layer, to, col))
 
     def rhs_z_copy(k, step):
         to = ahead(col, step)
@@ -177,7 +192,13 @@
 
     def inv_z_copy(k, step):
         to = ahead(col, step)
-        return remote(inv_stage.at[k, to], inv_full.at[k, col], inv_z_sem, k, step, (layer, row, to))
+        at = pl.ds(*inv_rows(k))
+        return remote(inv_stage.at[k, to, at], inv_full.at[k, col, at], inv_z_sem, k, step, (layer, row, to))
+
+    def inv_share_copy(k, step):
+        block = inv_full.at[k, :, pl.ds(*inv_rows(k))]
+        to = ahead(layer, step, layers)
+        return remote(block, block, share_sem, k // (LEVELS + 1), step, (to, row, col))
 
     mate = col + 1 - 2 * lax.rem(col, 2)
     keep, give = lax.rem(col + half, grid), lax.rem(mate + half, grid)
@@ -195,8 +216,6 @@
         return remote(
             cross.at[0], cross.at[step], cross_sem, 0, step, (ahead(layer, step, layers), row, col)
         )
-
-    rows = width // grid
 
     def out_z_copy(k, step):
         to = ahead(col, step)
@@ -231,7 +250,17 @@
 
     def inv_row(k):
         own_inv_copy(k).wait()
-        start(inv_copy, k)
+        for step in (1, 2):
+            copy = inv_copy(k, step)
+            copy.start()
+            sent.append(copy)
+
+    def inv_relay(k):
+        for step in (1, 2):
+            inv_copy(k, step).wait_recv()
+            copy = inv_relay_copy(k, step)
+            copy.start()
+            sent.append(copy)
 
     def rhs_col(k):
         arrive(rhs_copy, k)
@@ -239,9 +268,18 @@
         rhs_full[k, col] = rhs_stage[k, col]
 
     def inv_col(k):
-        arrive(inv_copy, k)
+        for step in (1, 2):
+            inv_relay_copy(k, step).wait_recv()
         start(inv_z_copy, k)
-        inv_full[k, col] = inv_stage[k, col]
+        at = pl.ds(*inv_rows(k))
+        inv_full[k, col, at] = inv_stage[k, col, at]
+
+    def inv_share(k):
+        arrive(inv_z_copy, k)
+        for step in range(1, layers):
+            copy = inv_share_copy(k, step)
+            copy.start()
+            sent.append(copy)
 
     def split(k):
         own_rhs_copy(k).wait()
@@ -253,7 +291,11 @@
         return rhs_full[k].reshape(width, columns)
 
     def apply_inverse(k, value):
-        arrive(inv_z_copy, k)
+        if k % (LEVELS + 1) == LEVELS:
+            for step in range(1, layers):
+                inv_share_copy(k, step).wait_recv()
+        else:
+            arrive(inv_z_copy, k)
         return dot(inv_full[k].reshape(width, width), pair(value))
 
     def couple(level, k, value, first, send):
@@ -311,10 +353,12 @@
         split(k)
     rhs_row(1)
     inv_row(1)
+    inv_relay(0)
     spread_coupling(1)
     rhs_col(0)
     inv_col(0)
     spread_coupling(2)
+    inv_relay(1)
     relay(0)
     rhs_col(1)
     inv_col(1)
@@ -325,6 +369,7 @@
     fore_zero_pair = pair(fore_zero)
     couple(0, 0, fore_zero_pair, True, True)
     relay(1)
+    inv_relay(2)
     spread_coupling(4)
     relay(2)
     spread_coupling(5)
@@ -343,11 +388,14 @@
     inv_row(6)
     relay(4)
     spread_coupling(7)
+    inv_relay(3)
     couple(2, 3, fore_zero_pair, True, False)
     rhs_col(3)
     inv_col(3)
     couple(2, 4, fore_one_pair, False, False)
     total = reduced(1)
+    inv_relay(7)
+    inv_relay(6)
     relay(5)
     fore_two = apply_inverse(2, right_side(2) - total)
     spread_coupling(8)
@@ -359,7 +407,11 @@
     inv_col(7)
     inv_col(6)
     relay(7)
+    inv_relay(5)
+    inv_relay(4)
     spread_coupling(10)
+    inv_share(3)
+    inv_share(7)
     rhs_last = right_side(3)
     cross[0] = reduced(2)
     for step in range(1, layers):
@@ -472,15 +524,16 @@
             pltpu.SemaphoreType.DMA((2, couplings, 4)),
             sems(levels),
             sems(levels),
+            pltpu.SemaphoreType.DMA((2, 2 * levels, 4)),
             sems(2 * levels),
-            sems(2 * levels),
+            sems(2, layers),
             sems(steps),
             sems(1, layers),
             sems(levels),
             sems(levels),
         ],
         compiler_params=pltpu.CompilerParams(
-            collective_id=0, has_side_effects=True, vmem_limit_bytes=48 * 2**20
+            collective_id=0, has_side_effects=True, vmem_limit_bytes=60 * 2**20
         ),
         cost_estimate=pl.CostEstimate(
             flops=2 * couplings * grid * width * width * columns,

time: 187 us -> 172 us (0.920); the launches traced: 186 us -> 169 us
  Pallas kernels: 173 us -> 164 us
  local copies, waits for them, and re-layouts: 12.2 us -> 3.82 us
    pallas_call x1, Pallas kernels: 173 us -> 164 us  [solve_in_kernel(): pl.pallas_call(functools.partial(kernel, layers, grid), out_shape=(jax.Sh...]
    unnamed x25 -> x7, local copies, waits for them, and re-layouts: 12.1 us -> 3.23 us
where the time goes in v4:
time: 172 us; the launch traced here: 169 us
  Pallas kernels  164 us (95%)
  local copies, waits for them, and re-layouts  3.82 us (2%)
    pallas_call x1, Pallas kernels, solve_in_kernel(): pl.pallas_call(functools.partial(kernel, layers, grid), out_shape=(jax.Sh...  164 us

profile of v4, /device:TPU:0, one launch (start us, length us, event | category | flops | bytes accessed | tf_op | source)
XLA Modules:
  0.0 168.8 jit_solution(18059030710555278686)
XLA Ops:
  0.6 0.0 copy-start.1
  0.6 0.7 copy-done.1
  1.3 0.1 copy.15
  1.4 0.6 reshape.43.pattern
  2.0 164.3 %shard_map.122 = (f32[3,64,512]{2,1,0:T(8,128)}, f32[64,512]{1,0:T(8,128)}) custom-call(s32[12]{0:T(128)} %reshape.43.pattern, f32[3,64,512]{2,1,0:T(8,128)} %bitcast.20, f32[64,512]{1,0:T(8,128)} %bitcast.24, f32[3,64,256]{2,1,0:T(8,128)} %bitcast.22, f32[64,256]{1,0:T(8,128)} %bitcast.26, f32[3,64,256]{2,1,0:T(8,128)} %bitcast.23, f32[64,256]{1,0:T(8,128)} %bitcast.27, ...), custom_call_target="tpu_custom_call" | custom-call | flops 805306368 | bytes 3145728 | tf_op jit(solution)/shard_map/pallas_call | solution.py:497
  166.3 0.0 copy-start
  166.3 1.8 %copy.19 = f32[1,3,1,1,64,512]{5,4,3,2,1,0:T(8,128)} copy(f32[1,3,1,1,64,512]{5,4,3,2,1,0:T(8,128)} %bitcast.21) | data formatting | bytes 786432
  168.1 0.0 copy-done
  168.1 0.7 copy.20
Async XLA Ops:
  0.6 0.7 copy-start.1
  166.3 1.8 %copy-start = (f32[64,512]{1,0:T(8,128)S(1)}, f32[64,512]{1,0:T(8,128)}, u32[]{:S(2)}) copy-start(f32[64,512]{1,0:T(8,128)} %get-tuple-element.5) | copy-start | bytes 393220

commit v5 on v4

--- a/solution.py
+++ b/solution.py
@@ -22,8 +22,10 @@
 
 def dot(a, paired):
     high, low = halves(a)
-    both = jnp.dot(high, paired, preferred_element_type=jnp.float32)
-    both = both + jnp.dot(low, paired, preferred_element_type=jnp.float32)
+    both = jnp.dot(
+        jnp.concatenate((high, low), axis=0), paired, preferred_element_type=jnp.float32
+    )
+    both = both[: a.shape[0]] + both[a.shape[0] :]
     columns = paired.shape[1] // 2
     return both[:, :columns] + both[:, columns:]
 
@@ -149,9 +151,11 @@
     above = lax.rem(row + half, grid)
     upper, lower = pl.ds(0, width // 2), pl.ds(width // 2, width // 2)
 
-    def coupling_copy(k, step):
+    def coupling_copy(k, step, second=False):
         to = (beside, above)[step - 1]
-        return remote(coupling.at[k, row], coupling.at[k, row], coupling_sem, k, step, (layer, to, col))
+        part_rows = (upper, lower)[(step - 1) ^ second]
+        block = coupling.at[k, row, part_rows]
+        return remote(block, block, coupling_sem, k, step + 4 * second, (layer, to, col))
 
     def relay_copy(k, step):
         come, to, part_rows = ((beside, above, upper), (above, beside, lower))[step - 1]
@@ -203,14 +207,18 @@
     mate = col + 1 - 2 * lax.rem(col, 2)
     keep, give = lax.rem(col + half, grid), lax.rem(mate + half, grid)
 
-    def give_copy(k):
-        return remote(part.at[k, give], given.at[k], part_sem, k, 1, (layer, row, mate))
+    def give_copy(k, at):
+        rows_at = (upper, lower)[at]
+        source = part.at[k, give, rows_at]
+        return remote(source, given.at[k, rows_at], part_sem, k, 1 + at, (layer, row, mate))
 
     def near_copy(k):
-        return remote(part.at[k, mate], arrived.at[k, 0], part_sem, k, 2, (layer, row, mate))
-
-    def far_copy(k):
-        return remote(part.at[k, keep], arrived.at[k, 1], part_sem, k, 3, (layer, row, keep))
+        return remote(part.at[k, mate], arrived.at[k, 0], part_sem, k, 3, (layer, row, mate))
+
+    def far_copy(k, at):
+        rows_at = (upper, lower)[at]
+        source = part.at[k, keep, rows_at]
+        return remote(source, arrived.at[k, 1, rows_at], part_sem, k, 4 + at, (layer, row, keep))
 
     def cross_copy(step):
         return remote(
@@ -237,12 +245,16 @@
         for step in others:
             make(k, step).wait_recv()
 
+    def spread_masked(k):
+        for second in (False, True):
+            for step in (1, 2):
+                copy = coupling_copy(k, step, second)
+                copy.start()
+                sent.append(copy)
+
     def spread_coupling(k):
         mask(k)
-        for step in (1, 2):
-            copy = coupling_copy(k, step)
-            copy.start()
-            sent.append(copy)
+        spread_masked(k)
 
     def rhs_row(k):
         start(rhs_copy, k)
@@ -300,6 +312,7 @@
 
     def couple(level, k, value, first, send):
         for step in (1, 2):
+            coupling_copy(k, step, True).wait_recv()
             relay_copy(k, step).wait_recv()
 
         def add(to):
@@ -318,20 +331,24 @@
             return
 
         add(give)
-        give_copy(level).start()
+        for at in (0, 1):
+            give_copy(level, at).start()
         add(mate)
         near_copy(level).start()
         add(keep)
-        give_copy(level).wait_recv()
-        part[level, keep] = part[level, keep] + given[level]
-        far_copy(level).start()
+        for at, rows_at in ((0, upper), (1, lower)):
+            give_copy(level, at).wait_recv()
+            part[level, keep, rows_at] = part[level, keep, rows_at] + given[level, rows_at]
+            far_copy(level, at).start()
+            sent.extend((give_copy(level, at), far_copy(level, at)))
         add(col)
-        sent.extend((give_copy(level), near_copy(level), far_copy(level)))
+        sent.append(near_copy(level))
 
     def reduced(level):
         near_copy(level).wait_recv()
         total = part[level, col] + arrived[level, 0]
-        far_copy(level).wait_recv()
+        for at in (0, 1):
+            far_copy(level, at).wait_recv()
         return total + arrived[level, 1]
 
     def emit(k, value):
@@ -344,17 +361,18 @@
         start(out_copy, k)
         out_full[k, row] = out_stage[k, row]
 
+    for k in range(LEVELS + 1):
+        split(k)
+    mask(0)
+    mask(1)
     pl.semaphore_wait(barrier, 2 * (grid - 1) + layers - 1)
-    split(0)
     rhs_row(0)
     inv_row(0)
-    spread_coupling(0)
-    for k in range(1, LEVELS + 1):
-        split(k)
+    spread_masked(0)
     rhs_row(1)
     inv_row(1)
     inv_relay(0)
-    spread_coupling(1)
+    spread_masked(1)
     rhs_col(0)
     inv_col(0)
     spread_coupling(2)
@@ -521,13 +539,13 @@
             pltpu.SemaphoreType.DMA((couplings,)),
             pltpu.SemaphoreType.DMA((levels,)),
             pltpu.SemaphoreType.DMA((2 * levels,)),
-            pltpu.SemaphoreType.DMA((2, couplings, 4)),
+            pltpu.SemaphoreType.DMA((2, couplings, 6)),
             sems(levels),
             sems(levels),
             pltpu.SemaphoreType.DMA((2, 2 * levels, 4)),
             sems(2 * levels),
             sems(2, layers),
-            sems(steps),
+            pltpu.SemaphoreType.DMA((2, steps, 5)),
             sems(1, layers),
             sems(levels),
             sems(levels),

time: 172 us -> 174 us (1.012); the launches traced: 169 us -> 174 us
  Pallas kernels: 164 us -> 169 us
    pallas_call x1, Pallas kernels: 164 us -> 169 us  [solve_in_kernel(): pl.pallas_call(functools.partial(kernel, layers, grid), out_shape=(jax.Sh...]
where the time goes in v5:
time: 174 us
  Pallas kernels  169 us (97%)
  local copies, waits for them, and re-layouts  3.82 us (2%)
    pallas_call x1, Pallas kernels, solve_in_kernel(): pl.pallas_call(functools.partial(kernel, layers, grid), out_shape=(jax.Sh...  169 us

profile of v5, /device:TPU:0, one launch (start us, length us, event | category | flops | bytes accessed | tf_op | source)
XLA Modules:
  0.0 173.5 jit_solution(8008558641189153260)
XLA Ops:
  0.6 0.0 copy-start.1
  0.6 0.7 copy-done.1
  1.3 0.1 copy.15
  1.4 0.6 reshape.43.pattern
  2.0 169.0 %shard_map.122 = (f32[3,64,512]{2,1,0:T(8,128)}, f32[64,512]{1,0:T(8,128)}) custom-call(s32[12]{0:T(128)} %reshape.43.pattern, f32[3,64,512]{2,1,0:T(8,128)} %bitcast.20, f32[64,512]{1,0:T(8,128)} %bitcast.24, f32[3,64,256]{2,1,0:T(8,128)} %bitcast.22, f32[64,256]{1,0:T(8,128)} %bitcast.26, f32[3,64,256]{2,1,0:T(8,128)} %bitcast.23, f32[64,256]{1,0:T(8,128)} %bitcast.27, ...), custom_call_target="tpu_custom_call" | custom-call | flops 805306368 | bytes 3145728 | tf_op jit(solution)/shard_map/pallas_call | solution.py:515
  171.0 0.0 copy-start
  171.0 1.8 %copy.19 = f32[1,3,1,1,64,512]{5,4,3,2,1,0:T(8,128)} copy(f32[1,3,1,1,64,512]{5,4,3,2,1,0:T(8,128)} %bitcast.21) | data formatting | bytes 786432
  172.8 0.0 copy-done
  172.9 0.7 copy.20
Async XLA Ops:
  0.6 0.7 copy-start.1
  171.0 1.8 %copy-start = (f32[64,512]{1,0:T(8,128)S(1)}, f32[64,512]{1,0:T(8,128)}, u32[]{:S(2)}) copy-start(f32[64,512]{1,0:T(8,128)} %get-tuple-element.5) | copy-start | bytes 393220

commit v6 on v4

--- a/solution.py
+++ b/solution.py
@@ -237,12 +237,15 @@
         for step in others:
             make(k, step).wait_recv()
 
-    def spread_coupling(k):
-        mask(k)
+    def spread_masked(k):
         for step in (1, 2):
             copy = coupling_copy(k, step)
             copy.start()
             sent.append(copy)
+
+    def spread_coupling(k):
+        mask(k)
+        spread_masked(k)
 
     def rhs_row(k):
         start(rhs_copy, k)
@@ -344,51 +347,53 @@
         start(out_copy, k)
         out_full[k, row] = out_stage[k, row]
 
+    split(0)
+    mask(0)
     pl.semaphore_wait(barrier, 2 * (grid - 1) + layers - 1)
-    split(0)
     rhs_row(0)
     inv_row(0)
-    spread_coupling(0)
+    spread_masked(0)
     for k in range(1, LEVELS + 1):
         split(k)
+    inv_relay(0)
+    rhs_col(0)
+    inv_col(0)
+    spread_coupling(1)
+    relay(0)
     rhs_row(1)
     inv_row(1)
-    inv_relay(0)
-    spread_coupling(1)
-    rhs_col(0)
-    inv_col(0)
     spread_coupling(2)
     inv_relay(1)
-    relay(0)
-    rhs_col(1)
-    inv_col(1)
+    relay(1)
     rhs_row(2)
     inv_row(2)
     spread_coupling(3)
     fore_zero = apply_inverse(0, right_side(0))
     fore_zero_pair = pair(fore_zero)
     couple(0, 0, fore_zero_pair, True, True)
-    relay(1)
+    rhs_col(1)
+    inv_col(1)
     inv_relay(2)
     spread_coupling(4)
     relay(2)
     spread_coupling(5)
+    couple(1, 1, fore_zero_pair, True, False)
+    relay(3)
     rhs_row(3)
     inv_row(3)
-    couple(1, 1, fore_zero_pair, True, False)
     total = reduced(0)
     rhs_col(2)
     inv_col(2)
     fore_one = apply_inverse(1, right_side(1) - total)
     fore_one_pair = pair(fore_one)
     couple(1, 2, fore_one_pair, False, True)
-    relay(3)
+    relay(4)
     spread_coupling(6)
+    inv_relay(3)
+    relay(5)
     inv_row(7)
     inv_row(6)
-    relay(4)
     spread_coupling(7)
-    inv_relay(3)
     couple(2, 3, fore_zero_pair, True, False)
     rhs_col(3)
     inv_col(3)
@@ -396,7 +401,6 @@
     total = reduced(1)
     inv_relay(7)
     inv_relay(6)
-    relay(5)
     fore_two = apply_inverse(2, right_side(2) - total)
     spread_coupling(8)
     couple(2, 5, pair(fore_two), False, True)

time: 172 us -> 169 us (0.983)
  Pallas kernels: 164 us -> 161 us
    pallas_call x1, Pallas kernels: 164 us -> 161 us  [solve_in_kernel(): pl.pallas_call(functools.partial(kernel, layers, grid), out_shape=(jax.Sh...]
where the time goes in v6:
time: 169 us; the launch traced here: 166 us
  Pallas kernels  161 us (95%)
  local copies, waits for them, and re-layouts  3.82 us (2%)
    pallas_call x1, Pallas kernels, solve_in_kernel(): pl.pallas_call(functools.partial(kernel, layers, grid), out_shape=(jax.Sh...  161 us

profile of v6, /device:TPU:0, one launch (start us, length us, event | category | flops | bytes accessed | tf_op | source)
XLA Modules:
  0.0 165.7 jit_solution(8368443734285778164)
XLA Ops:
  0.6 0.0 copy-start.1
  0.6 0.7 copy-done.1
  1.3 0.1 copy.15
  1.4 0.6 reshape.43.pattern
  2.0 161.2 %shard_map.122 = (f32[3,64,512]{2,1,0:T(8,128)}, f32[64,512]{1,0:T(8,128)}) custom-call(s32[12]{0:T(128)} %reshape.43.pattern, f32[3,64,512]{2,1,0:T(8,128)} %bitcast.20, f32[64,512]{1,0:T(8,128)} %bitcast.24, f32[3,64,256]{2,1,0:T(8,128)} %bitcast.22, f32[64,256]{1,0:T(8,128)} %bitcast.26, f32[3,64,256]{2,1,0:T(8,128)} %bitcast.23, f32[64,256]{1,0:T(8,128)} %bitcast.27, ...), custom_call_target="tpu_custom_call" | custom-call | flops 805306368 | bytes 3145728 | tf_op jit(solution)/shard_map/pallas_call | solution.py:501
  163.2 0.0 copy-start
  163.3 1.8 %copy.19 = f32[1,3,1,1,64,512]{5,4,3,2,1,0:T(8,128)} copy(f32[1,3,1,1,64,512]{5,4,3,2,1,0:T(8,128)} %bitcast.21) | data formatting | bytes 786432
  165.1 0.0 copy-done
  165.1 0.7 copy.20
Async XLA Ops:
  0.6 0.7 copy-start.1
  163.2 1.8 %copy-start = (f32[64,512]{1,0:T(8,128)S(1)}, f32[64,512]{1,0:T(8,128)}, u32[]{:S(2)}) copy-start(f32[64,512]{1,0:T(8,128)} %get-tuple-element.5) | copy-start | bytes 393220
